TPU v7x, 32 devices: a whole 2x2x4 slice. The times are simulated.
32 devices in a mesh: pipe: 2 (over y), dp: 4 (over z), tensor: 4 (over x, core).
Axes of the slice: x: 2, y: 2, z: 4, core: 2. Of those that a mesh axis runs over, the one named last changes fastest.
Arguments:
- tokens: bfloat16 [3072, 8192], P(('pipe', 'dp'), 'tensor'), parts along dimension 0, may hold values from -6 to 6
- pattern: int32 [128, 6], P('pipe'), parts along dimension 0, may hold values from 0 to 31, as said below
- blocks: bfloat16 [128, 6, 256, 256], P(('pipe', 'tensor'), None, 'dp'), parts along dimension 0, may hold values from -0.15625 to 0.15625
- left_factor: bfloat16 [16384, 512], P(('pipe', 'tensor'), 'dp'), parts along dimension 0, may hold values from -0.0625 to 0.0625
- right_factor: bfloat16 [1024, 16384], P(('pipe', 'dp'), 'tensor'), parts along dimension 0, may hold values from -0.25 to 0.25
- cotangent: bfloat16 [3072, 16384], P(('pipe', 'dp'), 'tensor'), parts along dimension 0, may hold values from -6 to 6
Outputs:
- hidden: bfloat16 [3072, 16384], P(('pipe', 'dp'), 'tensor'), parts along dimension 0
- token_grad: float32 [3072, 8192], P(('pipe', 'dp'), 'tensor'), parts along dimension 0
- block_grad: float32 [128, 6, 256, 256], P(('pipe', 'tensor'), None, 'dp'), parts along dimension 0
- left_grad: float32 [16384, 512], P(('pipe', 'tensor'), 'dp'), parts along dimension 0
- right_grad: float32 [1024, 16384], P(('pipe', 'dp'), 'tensor'), parts along dimension 0
There are 2 independent parts, one for each index of `pipe`. A program takes and returns all parts, laid end to end along the dimension named above; each array names one. Nothing has to cross between parts.
Inputs may be any that keep to these rules, and one draw needn't show every extreme that they name: `pattern`: row j lists the 6 input blocks feeding hidden block j: under a relabeling of the 32 input blocks drawn from the seed, they are the labels of (j mod 32) XOR s for s = 0 and then the powers of two below 32 in rising order; a row's entries are distinct.
All inputs are finite; a program needn't handle non-finite values.
Results may differ from a plain program's by a relative error of at most 0.017.
Values may be sent and summed in bfloat16 or wider, within the bound.
A program may use at most 256 MiB of HBM per device.

v0:
```python
import jax
import jax.numpy as jnp
from jax import lax
from jax.sharding import PartitionSpec as P

SQRT_HALF = 0.7071067811865476
INV_ROOT_TWO_PI = 0.3989422804014327


def gelu_parts(preact):
    normal_cdf = 0.5 * (1.0 + jax.scipy.special.erf(preact * SQRT_HALF))
    return (
        preact * normal_cdf,
        normal_cdf + preact * jnp.exp(-0.5 * preact * preact) * INV_ROOT_TWO_PI,
    )


def per_device(tokens, pattern, blocks, left_factor, right_factor, cotangent):
    tok_rows = tokens.shape[0]
    block_size = blocks.shape[3]
    local_cols = blocks.shape[0]
    slot_count = blocks.shape[1]
    full_tokens = lax.all_gather(tokens, "tensor", axis=1, tiled=True)
    block_count = full_tokens.shape[1] // block_size
    tensor_rank = lax.axis_index("tensor")
    local_pattern = lax.dynamic_slice_in_dim(pattern, tensor_rank * local_cols, local_cols, 0)
    picked = jnp.take(full_tokens.reshape(tok_rows, block_count, block_size), local_pattern, axis=1)
    inputs = picked
    butterfly = jnp.einsum(
        "tjkc,jkcd->tjd",
        inputs,
        lax.all_gather(blocks, "dp", axis=2, tiled=True),
        preferred_element_type=jnp.float32,
    )
    left_rows = lax.all_gather(left_factor, "dp", axis=1, tiled=True)
    whole_left = lax.all_gather(left_rows, "tensor", axis=0, tiled=True)
    rank_acts = jnp.dot(full_tokens, whole_left, preferred_element_type=jnp.float32).astype(
        jnp.bfloat16
    )
    inputs = rank_acts
    rank_part = jnp.dot(
        inputs,
        lax.all_gather(right_factor, "dp", axis=0, tiled=True),
        preferred_element_type=jnp.float32,
    )
    preact = butterfly.reshape(tok_rows, -1) + rank_part
    activated, slope_values = gelu_parts(preact)
    hidden = activated.astype(jnp.bfloat16)
    grad_pre = (cotangent.astype(jnp.float32) * slope_values).astype(jnp.bfloat16)
    rank_terms = lax.dot_general(
        grad_pre,
        lax.all_gather(right_factor, "dp", axis=0, tiled=True),
        (((1,), (1,)), ((), ())),
        preferred_element_type=jnp.float32,
    )
    rank_grad = lax.psum(rank_terms.astype(jnp.bfloat16), "tensor")
    right_term = lax.dot_general(
        rank_acts, grad_pre, (((0,), (0,)), ((), ())), preferred_element_type=jnp.float32
    )
    right_grad = lax.psum_scatter(
        right_term.astype(jnp.bfloat16), "dp", scatter_dimension=0, tiled=True
    ).astype(jnp.float32)
    left_term = lax.dot_general(
        tokens, rank_grad, (((0,), (0,)), ((), ())), preferred_element_type=jnp.float32
    )
    left_grad = lax.psum_scatter(
        left_term.astype(jnp.bfloat16), "dp", scatter_dimension=1, tiled=True
    ).astype(jnp.float32)
    grad_blocks = grad_pre.reshape(tok_rows, local_cols, block_size)
    block_term = jnp.einsum(
        "tjkc,tjd->jkcd", picked, grad_blocks, preferred_element_type=jnp.float32
    )
    block_grad = lax.psum_scatter(
        block_term.astype(jnp.bfloat16), "dp", scatter_dimension=2, tiled=True
    ).astype(jnp.float32)
    spread = jnp.einsum(
        "tjd,jkcd->tjkc",
        grad_blocks,
        lax.all_gather(blocks, "dp", axis=2, tiled=True),
        preferred_element_type=jnp.float32,
    )
    placed = (
        jnp.zeros((tok_rows, block_count, block_size), jnp.float32)
        .at[:, local_pattern.reshape(-1)]
        .add(spread.reshape(tok_rows, local_cols * slot_count, block_size))
    )
    token_part = lax.psum_scatter(
        placed.reshape(tok_rows, -1).astype(jnp.bfloat16), "tensor", scatter_dimension=1, tiled=True
    ).astype(jnp.float32)
    token_grad = token_part + lax.dot_general(
        rank_grad, left_rows, (((1,), (1,)), ((), ())), preferred_element_type=jnp.float32
    )
    return (hidden, token_grad, block_grad, left_grad, right_grad)


def solution(mesh):
    placed = (
        P(("pipe", "dp"), "tensor"),
        P("pipe", None),
        P(("pipe", "tensor"), None, "dp", None),
        P(("pipe", "tensor"), "dp"),
        P(("pipe", "dp"), "tensor"),
        P(("pipe", "dp"), "tensor"),
    )
    return jax.shard_map(
        per_device,
        mesh=mesh,
        in_specs=placed,
        out_specs=(
            P(("pipe", "dp"), "tensor"),
            P(("pipe", "dp"), "tensor"),
            P(("pipe", "tensor"), None, "dp", None),
            P(("pipe", "tensor"), "dp"),
            P(("pipe", "dp"), "tensor"),
        ),
        check_vma=False,
    )
```

profile of v0, /device:TPU:0, one launch (start us, length us, event | category | flops | bytes accessed | tf_op | source)
XLA Modules:
  0.0 936.8 jit_solution(5141369474184893608)
XLA Ops:
  7.2 0.0 copy-start.5
  7.2 0.0 all-gather.10.cloned.1.call-start
  7.2 0.7 all-gather.10.cloned.1.call-update
  7.9 0.0 all-gather.6.cloned.1.call-start
  8.0 2.6 copy.32
  10.5 0.0 all-gather.6.cloned.1.call-update
  10.6 0.0 all-gather.12.cloned.1.call-start
  10.6 47.9 %all-gather.10.cloned.1.call-done = bf16[2048,512]{1,0:T(8,128)(2,1)} async-done(((bf16[2048,128]{1,0:T(8,128)(2,1)}), bf16[2048,512]{1,0:T(8,128)(2,1)}) %all-gather.10.cloned.1.call-update) | async-done | bytes 2097168 | tf_op jit(solution)/shard_map/all_gather | solution.py:35
  58.5 0.0 all-gather.12.cloned.1.call-update
  58.6 0.0 all-gather.8.cloned.1.call-start
  58.6 0.5 all-gather.8.cloned.1.call-update
  59.1 0.0 all-gather.14.cloned.1.call-start
  59.2 0.5 all-gather.14.cloned.1.call-update
  59.7 0.0 all-reduce.2.cloned.1.call-start
  59.8 0.0 copy-done.5
  59.8 0.1 compare_and_fusion
  59.9 0.1 copy.31
  60.0 0.1 copy.33
  60.1 0.1 reshape.67
  60.2 45.2 %all-gather.6.cloned.1.call-done = bf16[384,8192]{0,1:T(8,128)(2,1)} async-done(((bf16[384,2048]{0,1:T(8,128)(2,1)}), bf16[384,8192]{0,1:T(8,128)(2,1)}) %all-gather.6.cloned.1.call-update) | async-done | bytes 6291472 | tf_op jit(solution)/shard_map/all_gather | solution.py:23
  105.3 8.6 copy.34
  114.0 13.0 %gather_fusion = bf16[96,384,256]{2,1,0:T(8,128)(2,1)} fusion(bf16[384,32,256]{2,0,1:T(8,128)(2,1)} %copy.34, s32[1024]{0:T(1024)S(1)} %pad_clamp_fusion), kind=kCustom, calls=%fused_computation | custom fusion | bytes 37749120 | tf_op jit(solution)/shard_map/jit(_take)/gather | solution.py:27
  126.9 24.7 %copy.35 = bf16[16,6,384,256]{2,3,1,0:T(8,128)(2,1)} copy(bf16[16,6,384,256]{3,2,1,0:T(8,128)(2,1)} %bitcast.47) | data formatting | bytes 37748736 | tf_op jit(solution)/shard_map/jit(_take)/gather | solution.py:27
  151.6 13.6 %all-gather.12.cloned.1.call-done = bf16[8192,512]{1,0:T(8,128)(2,1)} async-done(((bf16[2048,512]{1,0:T(8,128)(2,1)}), bf16[8192,512]{1,0:T(8,128)(2,1)}) %all-gather.12.cloned.1.call-update) | async-done | bytes 8388624 | tf_op jit(solution)/shard_map/all_gather | solution.py:36
  165.2 8.6 convolution_convert_fusion.3
  173.8 211.0 %all-gather.8.cloned.1.call-done = bf16[16,6,256,256]{3,2,1,0:T(8,128)(2,1)} async-done(((bf16[16,6,64,256]{3,2,1,0:T(8,128)(2,1)}), bf16[16,6,256,256]{3,2,1,0:T(8,128)(2,1)}) %all-gather.8.cloned.1.call-update) | async-done | bytes 12582928 | tf_op jit(solution)/shard_map/all_gather | solution.py:32
  384.9 16.6 %fusion.2 = f32[16,384,256,1]{1,2,3,0:T(8,128)} fusion(bf16[16,6,256,256]{3,2,1,0:T(8,128)(2,1)} %all-gather.8.cloned.1.call-done, bf16[16,6,384,256]{2,3,1,0:T(8,128)(2,1)} %copy.35, pred[16,6]{1,0:T(8,128)(4,1)S(1)} %copy.31), kind=kOutput, calls=%fused_computation.4 | convolution fusion | flops 4841275392 | bytes 37748832 | tf_op jit(solution)/shard_map/tjkc,jkcd->tjd/dot_general | solution.py:29
  401.5 6.6 copy.37
  408.1 57.2 %all-gather.14.cloned.1.call-done = bf16[512,4096]{1,0:T(8,128)(2,1)} async-done(((bf16[128,4096]{1,0:T(8,128)(2,1)}), bf16[512,4096]{1,0:T(8,128)(2,1)}) %all-gather.14.cloned.1.call-update) | async-done | bytes 4194320 | tf_op jit(solution)/shard_map/all_gather | solution.py:43
  465.3 10.5 %fusion.14 = (bf16[384,4096]{1,0:T(8,128)(2,1)S(1)}, bf16[384,4096]{1,0:T(8,128)(2,1)}) fusion(bf16[384,4096]{1,0:T(8,128)(2,1)} %param.11, f32[384,4096]{1,0:T(8,128)} %copy.37, bf16[384,512]{1,0:T(8,128)(2,1)S(1)} %convolution_convert_fusion.3, bf16[512,4096]{1,0:T(8,128)(2,1)} %all-gather.14.cloned.1.call-done), kind=kOutput, calls=%fused_computation.16 | convolution fusion | flops 1632632832 | bytes 20316160 | tf_op jit(solution)/shard_map/dot_general | solution.py:41
  475.8 0.0 copy-done.6
  475.8 2.6 convolution_convert_fusion.2
  478.5 0.0 all-reduce.2.cloned.1.call-update
  478.5 0.2 reduce-scatter.9.cloned.1.call-start
  478.7 31.1 %all-reduce.2.cloned.1.call-done = bf16[384,512]{1,0:T(8,128)(2,1)} async-done(((bf16[384,512]{1,0:T(8,128)(2,1)}), bf16[384,512]{1,0:T(8,128)(2,1)}) %all-reduce.2.cloned.1.call-update) | async-done | bytes 393232 | tf_op jit(solution)/shard_map/psum | solution.py:56
  509.8 4.1 fusion.18
  513.9 0.0 reduce-scatter.9.cloned.1.call-update
  513.9 0.0 reduce-scatter.11.cloned.1.call-start
  514.0 0.0 copy-done.2
  514.0 4.4 convolution_convert_fusion
  518.4 0.0 reduce-scatter.11.cloned.1.call-update
  518.5 0.0 reduce-scatter.5.cloned.1.call-start
  518.5 0.1 copy.38
  518.6 0.1 reshape.62
  518.7 3.3 copy.52
  522.0 0.0 copy-start
  522.0 25.2 %fusion.16 = f32[16,384,6,256]{3,1,2,0:T(8,128)} fusion(bf16[16,6,256,256]{3,2,1,0:T(8,128)(2,1)} %all-gather.8.cloned.1.call-done, bf16[384,16,256,1]{2,1,0,3:T(8,128)(2,1)S(1)} %bitcast.50), kind=kOutput, calls=%fused_computation.25 | convolution fusion | flops 4831838208 | bytes 53477376 | tf_op jit(solution)/shard_map/tjd,jkcd->tjkc/dot_general | solution.py:76
  547.2 0.0 copy-done
  547.2 5.9 broadcast_in_dim.19
  553.1 90.2 %scatter_fusion = f32[384,32,256]{2,0,1:T(8,128)} fusion(f32[384,32,256]{2,0,1:T(8,128)} %broadcast_in_dim.19, s32[96]{0:T(128)S(1)} %fusion.19, f32[96,384,256]{2,1,0:T(8,128)} %bitcast.46), kind=kCustom, calls=%fused_computation.1 | custom fusion | flops 9437184 | bytes 113246592 | tf_op jit(solution)/shard_map/scatter-add | solution.py:85
  643.3 5.4 convert_bitcast_fusion
  648.8 3.5 copy.51
  652.3 0.0 reduce-scatter.5.cloned.1.call-update
  652.3 0.3 reduce-scatter.7.cloned.1.call-start
  652.6 1.6 copy-done.1
  654.2 15.2 %fusion.6 = bf16[16,6,256,256]{3,2,1,0:T(8,128)(2,1)} fusion(bf16[16,6,384,256]{2,3,1,0:T(8,128)(2,1)} %copy.35, pred[16,6]{1,0:T(8,128)(4,1)S(1)} %copy.31, bf16[384,16,256,1]{2,1,0,3:T(8,128)(2,1)S(1)} %bitcast.51), kind=kOutput, calls=%fused_computation.10 | convolution fusion | flops 4847566848 | bytes 34603104 | tf_op jit(solution)/shard_map/tjkc,tjd->jkcd/dot_general | solution.py:70
  669.4 0.0 reduce-scatter.7.cloned.1.call-update
  669.5 0.0 reduce-scatter.9.cloned.1.call-done
  669.5 2.4 copy.42
  671.9 2.9 convert_element_type.59
  674.8 35.7 %reduce-scatter.5.cloned.1.call-done = bf16[384,2048]{1,0:T(8,128)(2,1)} async-done(((bf16[384,8192]{1,0:T(8,128)(2,1)}), bf16[384,2048]{1,0:T(8,128)(2,1)}) %reduce-scatter.5.cloned.1.call-update) | async-done | bytes 1572880 | tf_op jit(solution)/shard_map/reduce_scatter | solution.py:87
  710.4 4.1 convert_add_fusion
  714.5 210.0 %reduce-scatter.7.cloned.1.call-done = bf16[16,6,64,256]{3,2,1,0:T(8,128)(2,1)} async-done(((bf16[16,6,256,256]{3,2,1,0:T(8,128)(2,1)}), bf16[16,6,64,256]{3,2,1,0:T(8,128)(2,1)}) %reduce-scatter.7.cloned.1.call-update) | async-done | bytes 3145744 | tf_op jit(solution)/shard_map/reduce_scatter | solution.py:73
  924.5 5.5 convert_element_type.54
  (11 shorter events, 0.0 us)
Async XLA Ops:
  7.2 52.6 %copy-start.5 = (s32[64,6]{0,1:T(8,128)S(1)}, s32[64,6]{0,1:T(8,128)}, u32[]{:S(2)}) copy-start(s32[64,6]{0,1:T(8,128)} %param.7) | copy-start | bytes 4612
  7.2 51.4 %all-gather.10.cloned.1.call-start = ((), (), s32[]{:S(2)}) async-start(), calls=%async_computation.6 | async-start | bytes 2621440 | tf_op jit(solution)/shard_map/all_gather | solution.py:35
  7.9 97.4 %all-gather.6.cloned.1.call-start = ((), (), s32[]{:S(2)}) async-start(), calls=%async_computation.4 | async-start | bytes 7864320 | tf_op jit(solution)/shard_map/all_gather | solution.py:23
  10.6 154.6 %all-gather.12.cloned.1.call-start = ((), (), s32[]{:S(2)}) async-start(), calls=%async_computation.7 | async-start | bytes 10485760 | tf_op jit(solution)/shard_map/all_gather | solution.py:36
  58.6 326.3 %all-gather.8.cloned.1.call-start = ((), (), s32[]{:S(2)}) async-start(), calls=%async_computation.5 | async-start | bytes 15728640 | tf_op jit(solution)/shard_map/all_gather | solution.py:32
  59.1 406.1 %all-gather.14.cloned.1.call-start = ((), (), s32[]{:S(2)}) async-start(), calls=%async_computation.8 | async-start | bytes 5242880 | tf_op jit(solution)/shard_map/all_gather | solution.py:43
  59.7 450.0 %all-reduce.2.cloned.1.call-start = ((), (), s32[]{:S(2)}) async-start(), calls=%async_computation.10 | async-start | bytes 786432 | tf_op jit(solution)/shard_map/psum | solution.py:56
  465.3 10.5 %copy-start.6 = (bf16[512,4096]{1,0:T(8,128)(2,1)S(1)}, bf16[512,4096]{1,0:T(8,128)(2,1)}, u32[]{:S(2)}) copy-start(bf16[512,4096]{1,0:T(8,128)(2,1)} %all-gather.14.cloned.1.call-done) | copy-start | bytes 12582916
  475.8 38.2 %copy-start.2 = (bf16[384,4096]{1,0:T(8,128)(2,1)}, bf16[384,4096]{1,0:T(8,128)(2,1)S(1)}, u32[]{:S(2)}) copy-start(bf16[384,4096]{1,0:T(8,128)(2,1)S(1)} %get-tuple-element.22) | copy-start | bytes 9437188
  478.5 191.0 %reduce-scatter.9.cloned.1.call-start = ((), (), s32[]{:S(2)}) async-start(), calls=%async_computation.12 | async-start | bytes 2621440 | tf_op jit(solution)/shard_map/reduce_scatter | solution.py:66
  513.9 157.9 %reduce-scatter.11.cloned.1.call-start = ((), (), s32[]{:S(2)}) async-start(), calls=%async_computation.13 | async-start | bytes 5242880 | tf_op jit(solution)/shard_map/reduce_scatter | solution.py:60
  518.5 192.0 %reduce-scatter.5.cloned.1.call-start = ((), (), s32[]{:S(2)}) async-start(), calls=%async_computation.9 | async-start | bytes 7864320 | tf_op jit(solution)/shard_map/reduce_scatter | solution.py:87
  522.0 25.2 %copy-start = (bf16[48,8,16,256]{3,2,1,0:T(8,128)(2,1)}, bf16[48,8,16,256]{3,2,1,0:T(8,128)(2,1)S(1)}, u32[]{:S(2)}) copy-start(bf16[48,8,16,256]{3,2,1,0:T(8,128)(2,1)S(1)} %copy.52) | copy-start | bytes 9437188
  652.3 1.9 copy-start.1
  652.3 272.2 %reduce-scatter.7.cloned.1.call-start = ((), (), s32[]{:S(2)}) async-start(), calls=%async_computation.11 | async-start | bytes 15728640 | tf_op jit(solution)/shard_map/reduce_scatter | solution.py:73
  669.4 41.0 %copy-start.3 = (bf16[2048,512]{1,0:T(8,128)(2,1)S(1)}, bf16[2048,512]{1,0:T(8,128)(2,1)}, u32[]{:S(2)}) copy-start(bf16[2048,512]{1,0:T(8,128)(2,1)} %all-gather.10.cloned.1.call-done) | copy-start | bytes 6291460
  669.4 41.0 %copy-start.4 = (bf16[384,512]{1,0:T(8,128)(2,1)S(1)}, bf16[384,512]{1,0:T(8,128)(2,1)}, u32[]{:S(2)}) copy-start(bf16[384,512]{1,0:T(8,128)(2,1)} %all-reduce.2.cloned.1.call-done) | copy-start | bytes 1179652
Sparse Core Ops, SparseCore 0:
  9.6 48.9 all-gather.9
  60.7 44.5 all-gather.5
  106.9 58.2 all-gather.11
  166.6 218.2 all-gather.7
  386.3 78.9 all-gather.13
  478.6 31.1 all-reduce.1
  514.0 43.8 reduce-scatter.8
  560.2 76.0 reduce-scatter.10
  652.4 57.9 reduce-scatter.4
  712.6 211.8 reduce-scatter.6
where the time goes:
time: 939 us; the launch traced here: 937 us
  waiting for transfers between devices  654 us (70%)
  other arithmetic  104 us (11%)
  matrix products  91.5 us (10%)
  local copies, waits for them, and re-layouts  72.6 us (8%)
  between operations  14.3 us (2%)
    all_gather x1, waiting for transfers between devices, per_device(): lax.all_gather(blocks, 'dp', axis=2, tiled=True)  211 us
    reduce_scatter x1, waiting for transfers between devices, per_device(): lax.psum_scatter(block_term.astype(jnp.bfloat16), 'dp', scatter_dimension...  210 us
    scatter-add x1, other arithmetic, per_device(): placed = jnp.zeros((tok_rows, block_count, block_size), jnp.float32).at[:...  90.2 us
    all_gather x1, waiting for transfers between devices, per_device(): lax.all_gather(right_factor, 'dp', axis=0, tiled=True)  57.2 us
    all_gather x1, waiting for transfers between devices, per_device(): left_rows = lax.all_gather(left_factor, 'dp', axis=1, tiled=True)  47.9 us
    all_gather x1, waiting for transfers between devices, per_device(): full_tokens = lax.all_gather(tokens, 'tensor', axis=1, tiled=True)  45.2 us
    gather x2, local copies, waits for them, and re-layouts, per_device(): jnp.take(full_tokens.reshape(tok_rows, block_count, block_size), local_pa...  37.6 us
    reduce_scatter x1, waiting for transfers between devices, per_device(): lax.psum_scatter(placed.reshape(tok_rows, -1).astype(jnp.bfloat16), 'tens...  35.7 us
  transfers between devices with their start and end apart: 10, of which 8 were waited for; matrix products, arithmetic and copies ran while one was open for 26% of the time, Pallas kernels for 0%

commit v1 on v0

--- a/solution.py
+++ b/solution.py
@@ -26,12 +26,37 @@
     local_pattern = lax.dynamic_slice_in_dim(pattern, tensor_rank * local_cols, local_cols, 0)
     picked = jnp.take(full_tokens.reshape(tok_rows, block_count, block_size), local_pattern, axis=1)
     inputs = picked
+    peers, mine, rows = (lax.axis_size("dp"), lax.axis_index("dp"), blocks.shape[2])
+    right = [(i, (i + 1) % peers) for i in range(peers)]
+    backward = [(i, (i - 1) % peers) for i in range(peers)]
+    middle = peers // 2
+    from_left = from_right = blocks
     butterfly = jnp.einsum(
         "tjkc,jkcd->tjd",
-        inputs,
-        lax.all_gather(blocks, "dp", axis=2, tiled=True),
+        lax.dynamic_slice_in_dim(inputs, mine * rows, blocks.shape[2], axis=3),
+        blocks,
         preferred_element_type=jnp.float32,
     )
+    for step in range(1, middle + 1):
+        from_left = lax.ppermute(from_left, "dp", right)
+        if step < peers - middle:
+            from_right = lax.ppermute(from_right, "dp", backward)
+            butterfly = butterfly + jnp.einsum(
+                "tjkc,jkcd->tjd",
+                lax.dynamic_slice_in_dim(
+                    inputs, (mine + step) % peers * rows, from_right.shape[2], axis=3
+                ),
+                from_right,
+                preferred_element_type=jnp.float32,
+            )
+        butterfly = butterfly + jnp.einsum(
+            "tjkc,jkcd->tjd",
+            lax.dynamic_slice_in_dim(
+                inputs, (mine - step) % peers * rows, from_left.shape[2], axis=3
+            ),
+            from_left,
+            preferred_element_type=jnp.float32,
+        )
     left_rows = lax.all_gather(left_factor, "dp", axis=1, tiled=True)
     whole_left = lax.all_gather(left_rows, "tensor", axis=0, tiled=True)
     rank_acts = jnp.dot(full_tokens, whole_left, preferred_element_type=jnp.float32).astype(

time: 939 us -> 1040 us (1.11)
  waiting for transfers between devices: 654 us -> 730 us
  other arithmetic: 104 us -> 118 us
    ppermute x0 -> x3, waiting for transfers between devices: none -> 192 us  [the longest x2 142 us: per_device(): from_left = lax.ppermute(from_left, 'dp', right)]
    all_gather x1, waiting for transfers between devices: 57.2 us -> 0.02 us  [per_device(): lax.all_gather(right_factor, 'dp', axis=0, tiled=True)]
    all_gather x1, waiting for transfers between devices: 45.2 us -> 0.01 us  [per_device(): full_tokens = lax.all_gather(tokens, 'tensor', axis=1, tiled=True)]
    dot_general x1 -> x4, matrix products: 16.6 us -> 34.8 us  [the longest x2 22.8 us: per_device(): jnp.einsum('tjkc,jkcd->tjd', lax.dynamic_slice_in_dim(inputs, (mine - ste...]
    all_gather x1, waiting for transfers between devices: 13.6 us -> 0.01 us  [per_device(): whole_left = lax.all_gather(left_rows, 'tensor', axis=0, tiled=True)]
  transfers between devices with their start and end apart: 10 -> 13, of which waited for: 8 -> 8; matrix products, arithmetic and copies ran while one was open for 26% -> 26% of each run, Pallas kernels for 0% -> 0%
where the time goes in v1:
time: 1040 us
  waiting for transfers between devices  730 us (70%)
  other arithmetic  118 us (11%)
  matrix products  96.8 us (9%)
  local copies, waits for them, and re-layouts  72.4 us (7%)
  between operations  14.3 us (1%)
    reduce_scatter x1, waiting for transfers between devices, per_device(): lax.psum_scatter(block_term.astype(jnp.bfloat16), 'dp', scatter_dimension...  210 us
    all_gather x1, waiting for transfers between devices, per_device(): lax.all_gather(blocks, 'dp', axis=2, tiled=True)  208 us
    ppermute x2, waiting for transfers between devices, per_device(): from_left = lax.ppermute(from_left, 'dp', right)  142 us
    scatter-add x1, other arithmetic, per_device(): placed = jnp.zeros((tok_rows, block_count, block_size), jnp.float32).at[:...  90.1 us
    ppermute x1, waiting for transfers between devices, per_device(): from_right = lax.ppermute(from_right, 'dp', backward)  50.4 us
    all_gather x1, waiting for transfers between devices, per_device(): left_rows = lax.all_gather(left_factor, 'dp', axis=1, tiled=True)  47.8 us
    reduce_scatter x1, waiting for transfers between devices, per_device(): lax.psum_scatter(placed.reshape(tok_rows, -1).astype(jnp.bfloat16), 'tens...  39.3 us
    gather x2, local copies, waits for them, and re-layouts, per_device(): jnp.take(full_tokens.reshape(tok_rows, block_count, block_size), local_pa...  36.7 us
  transfers between devices with their start and end apart: 13, of which 8 were waited for; matrix products, arithmetic and copies ran while one was open for 26% of the time, Pallas kernels for 0%

profile of v1, /device:TPU:0, one launch (start us, length us, event | category | flops | bytes accessed | tf_op | source)
XLA Modules:
  0.0 1036.4 jit_solution(3268159570057184022)
XLA Ops:
  7.2 0.0 all-gather.8.cloned.1.call-start
  7.2 0.7 all-gather.8.cloned.1.call-update
  7.9 0.0 all-gather.6.cloned.1.call-start
  8.0 2.7 copy.29
  10.7 0.0 all-gather.6.cloned.1.call-update
  10.7 0.0 all-gather.10.cloned.1.call-start
  10.8 47.8 %all-gather.8.cloned.1.call-done = bf16[2048,512]{1,0:T(8,128)(2,1)} async-done(((bf16[2048,128]{1,0:T(8,128)(2,1)}), bf16[2048,512]{1,0:T(8,128)(2,1)}) %all-gather.8.cloned.1.call-update) | async-done | bytes 2097168 | tf_op jit(solution)/shard_map/all_gather | solution.py:60
  58.6 0.0 all-gather.10.cloned.1.call-update
  58.6 0.0 all-gather.12.cloned.1.call-start
  58.6 0.2 collective-permute-start.1
  58.9 0.3 all-gather.12.cloned.1.call-update
  59.2 0.0 all-reduce.2.cloned.1.call-start
  59.2 3.4 collective-permute-start
  62.6 0.1 compare_and_fusion
  62.7 0.1 copy.28
  62.8 0.1 copy.30
  62.9 0.1 reshape.67
  63.0 68.6 %collective-permute-done.1 = bf16[16,6,64,256]{3,2,1,0:T(8,128)(2,1)} collective-permute-done((bf16[16,6,64,256]{3,2,1,0:T(8,128)(2,1)S(1)}, bf16[16,6,64,256]{3,2,1,0:T(8,128)(2,1)}, u32[]{:S(2)}, u32[]{:S(2)}) %collective-permute-start.1) | collective-permute-done | bytes 3145760 | tf_op jit(solution)/shard_map/ppermute | solution.py:41
  131.6 8.6 copy.31
  140.2 12.0 %gather_fusion = bf16[96,384,256]{2,1,0:T(8,128)(2,1)} fusion(bf16[384,32,256]{2,0,1:T(8,128)(2,1)} %copy.31, s32[1024]{0:T(1024)S(1)} %pad_clamp_fusion), kind=kCustom, calls=%fused_computation | custom fusion | bytes 37749120 | tf_op jit(solution)/shard_map/jit(_take)/gather | solution.py:27
  152.2 24.7 %copy.32 = bf16[96,384,256]{1,2,0:T(8,128)(2,1)} copy(bf16[96,384,256]{2,1,0:T(8,128)(2,1)} %gather_fusion) | data formatting | bytes 37748736 | tf_op jit(solution)/shard_map/jit(_take)/gather | solution.py:27
  177.0 10.3 broadcast_select_fusion
  187.3 5.3 fusion.17
  192.6 9.1 fusion.13
  201.7 50.4 %collective-permute-done = bf16[16,6,64,256]{3,2,1,0:T(8,128)(2,1)} collective-permute-done((bf16[16,6,64,256]{3,2,1,0:T(8,128)(2,1)S(1)}, bf16[16,6,64,256]{3,2,1,0:T(8,128)(2,1)}, u32[]{:S(2)}, u32[]{:S(2)}) %collective-permute-start) | collective-permute-done | bytes 3145760 | tf_op jit(solution)/shard_map/ppermute | solution.py:43
  252.1 6.7 fusion.15
  258.8 73.2 %collective-permute-done.2 = bf16[16,6,64,256]{3,2,1,0:T(8,128)(2,1)} collective-permute-done((bf16[16,6,64,256]{3,2,1,0:T(8,128)(2,1)}, bf16[16,6,64,256]{3,2,1,0:T(8,128)(2,1)}, u32[]{:S(2)}, u32[]{:S(2)}) %collective-permute-start.2) | collective-permute-done | bytes 3145760 | tf_op jit(solution)/shard_map/ppermute | solution.py:41
  332.0 13.6 %bitcast_add_fusion = f32[16,384,256]{1,2,0:T(8,128)} fusion(f32[16,384,256,1]{1,2,3,0:T(8,128)} %fusion.13, f32[16,384,256,1]{1,2,3,0:T(8,128)} %fusion.15, f32[16,384,256,1]{1,2,3,0:T(8,128)} %fusion.17, bf16[16,6,64,256]{3,2,1,0:T(8,128)(2,1)} %collective-permute-done.2, bf16[16,6,384,256]{2,3,1,0:T(8,128)(2,1)} %copy-done, s32[]{:T(128)S(6)} %select_n.58), kind=kOutput, calls=%fused_computation.13 | convolution fusion | flops 1212678144 | bytes 33030148 | tf_op jit(solution)/shard_map/tjkc,jkcd->tjd/dot_general | solution.py:52
  345.7 6.6 copy.33
  352.3 8.6 convolution_convert_fusion.3
  361.0 0.0 all-gather.12.cloned.1.call-done
  361.0 4.1 fusion.34
  365.2 0.8 copy-done.6
  366.0 4.2 fusion.10
  370.2 2.6 convolution_convert_fusion.2
  372.8 0.0 all-gather.14.cloned.1.call-start
  372.8 0.5 all-gather.14.cloned.1.call-update
  373.4 0.0 reduce-scatter.9.cloned.1.call-start
  373.4 31.2 %all-reduce.2.cloned.1.call-done = bf16[384,512]{1,0:T(8,128)(2,1)} async-done(((bf16[384,512]{1,0:T(8,128)(2,1)}), bf16[384,512]{1,0:T(8,128)(2,1)}) %all-reduce.2.cloned.1.call-update) | async-done | bytes 393232 | tf_op jit(solution)/shard_map/psum | solution.py:81
  404.6 4.1 fusion.26
  408.8 0.0 reduce-scatter.11.cloned.1.call-start
  408.8 4.4 convolution_convert_fusion
  413.2 0.0 reduce-scatter.11.cloned.1.call-update
  413.2 0.0 reduce-scatter.5.cloned.1.call-start
  413.3 0.1 copy.34
  413.4 0.1 reshape.62
  413.5 2.8 copy.50
  416.2 208.2 %all-gather.14.cloned.1.call-done = bf16[16,6,256,256]{3,2,1,0:T(8,128)(2,1)} async-done(((bf16[16,6,64,256]{3,2,1,0:T(8,128)(2,1)}), bf16[16,6,256,256]{3,2,1,0:T(8,128)(2,1)}) %all-gather.14.cloned.1.call-update) | async-done | bytes 12582928 | tf_op jit(solution)/shard_map/all_gather | solution.py:104
  624.4 20.3 %fusion.24 = f32[16,384,6,256]{3,1,2,0:T(8,128)} fusion(bf16[16,6,256,256]{3,2,1,0:T(8,128)(2,1)} %all-gather.14.cloned.1.call-done, bf16[384,16,256,1]{2,1,0,3:T(8,128)(2,1)} %bitcast.80), kind=kOutput, calls=%fused_computation.35 | convolution fusion | flops 4831838208 | bytes 53477376 | tf_op jit(solution)/shard_map/tjd,jkcd->tjkc/dot_general | solution.py:101
  644.7 6.0 broadcast_in_dim.19
  650.7 90.1 %scatter_fusion = f32[384,32,256]{2,0,1:T(8,128)} fusion(f32[384,32,256]{2,0,1:T(8,128)} %broadcast_in_dim.19, s32[96]{0:T(128)S(1)} %fusion.33, f32[96,384,256]{2,1,0:T(8,128)} %bitcast.74), kind=kCustom, calls=%fused_computation.1 | custom fusion | flops 9437184 | bytes 113246592 | tf_op jit(solution)/shard_map/scatter-add | solution.py:110
  740.8 5.5 convert_bitcast_fusion
  746.3 3.5 copy.49
  749.8 0.0 reduce-scatter.7.cloned.1.call-start
  749.9 1.8 copy-done.2
  751.7 13.8 %fusion.2 = bf16[16,6,256,256]{3,2,1,0:T(8,128)(2,1)} fusion(bf16[16,6,384,256]{2,3,1,0:T(8,128)(2,1)} %copy-done, bf16[384,16,256,1]{2,1,0,3:T(8,128)(2,1)S(1)} %bitcast.81), kind=kOutput, calls=%fused_computation.6 | convolution fusion | flops 4838129664 | bytes 34603008 | tf_op jit(solution)/shard_map/tjkc,tjd->jkcd/dot_general | solution.py:95
  765.5 0.0 reduce-scatter.7.cloned.1.call-update
  765.5 0.0 reduce-scatter.9.cloned.1.call-done
  765.6 2.4 copy.38
  767.9 2.8 convert_element_type.59
  770.7 39.3 %reduce-scatter.5.cloned.1.call-done = bf16[384,2048]{1,0:T(8,128)(2,1)} async-done(((bf16[384,8192]{1,0:T(8,128)(2,1)}), bf16[384,2048]{1,0:T(8,128)(2,1)}) %reduce-scatter.5.cloned.1.call-update) | async-done | bytes 1572880 | tf_op jit(solution)/shard_map/reduce_scatter | solution.py:112
  810.0 4.1 convert_add_fusion
  814.1 210.0 %reduce-scatter.7.cloned.1.call-done = bf16[16,6,64,256]{3,2,1,0:T(8,128)(2,1)} async-done(((bf16[16,6,256,256]{3,2,1,0:T(8,128)(2,1)}), bf16[16,6,64,256]{3,2,1,0:T(8,128)(2,1)}) %reduce-scatter.7.cloned.1.call-update) | async-done | bytes 3145744 | tf_op jit(solution)/shard_map/reduce_scatter | solution.py:98
  1024.1 5.5 convert_element_type.54
  (26 shorter events, 0.1 us)
Async XLA Ops:
  7.2 51.5 %copy-start.3 = (bf16[16,6,64,256]{3,2,1,0:T(8,128)(2,1)S(1)}, bf16[16,6,64,256]{3,2,1,0:T(8,128)(2,1)}, u32[]{:S(2)}) copy-start(bf16[16,6,64,256]{3,2,1,0:T(8,128)(2,1)} %param.8) | copy-start | bytes 9437188
  7.2 55.5 %copy-start.8 = (s32[64,6]{0,1:T(8,128)S(1)}, s32[64,6]{0,1:T(8,128)}, u32[]{:S(2)}) copy-start(s32[64,6]{0,1:T(8,128)} %param.7) | copy-start | bytes 4612
  7.2 51.4 %all-gather.8.cloned.1.call-start = ((), (), s32[]{:S(2)}) async-start(), calls=%async_computation.5 | async-start | bytes 2621440 | tf_op jit(solution)/shard_map/all_gather | solution.py:60
  7.9 123.7 %all-gather.6.cloned.1.call-start = ((), (), s32[]{:S(2)}) async-start(), calls=%async_computation.4 | async-start | bytes 7864320 | tf_op jit(solution)/shard_map/all_gather | solution.py:23
  10.7 341.6 %all-gather.10.cloned.1.call-start = ((), (), s32[]{:S(2)}) async-start(), calls=%async_computation.6 | async-start | bytes 10485760 | tf_op jit(solution)/shard_map/all_gather | solution.py:61
  58.6 302.4 %all-gather.12.cloned.1.call-start = ((), (), s32[]{:S(2)}) async-start(), calls=%async_computation.7 | async-start | bytes 5242880 | tf_op jit(solution)/shard_map/all_gather | solution.py:68
  58.6 73.0 %collective-permute-start.1 = (bf16[16,6,64,256]{3,2,1,0:T(8,128)(2,1)S(1)}, bf16[16,6,64,256]{3,2,1,0:T(8,128)(2,1)}, u32[]{:S(2)}, u32[]{:S(2)}) collective-permute-start(bf16[16,6,64,256]{3,2,1,0:T(8,128)(2,1)S(1)} %copy-done.3), channel_id=1, source_target_pairs={{0,4},{4,8},{8,12},{12,0},{1,5},{5,9},{9,13},{13,1},{2,6},{6,10},{... | collective-permute-start | bytes 9437192 | tf_op jit(solution)/shard_map/ppermute | solution.py:41
  59.2 345.5 %all-reduce.2.cloned.1.call-start = ((), (), s32[]{:S(2)}) async-start(), calls=%async_computation.10 | async-start | bytes 786432 | tf_op jit(solution)/shard_map/psum | solution.py:81
  59.2 192.9 %collective-permute-start = (bf16[16,6,64,256]{3,2,1,0:T(8,128)(2,1)S(1)}, bf16[16,6,64,256]{3,2,1,0:T(8,128)(2,1)}, u32[]{:S(2)}, u32[]{:S(2)}) collective-permute-start(bf16[16,6,64,256]{3,2,1,0:T(8,128)(2,1)S(1)} %copy-done.3), channel_id=1, source_target_pairs={{0,12},{4,0},{8,4},{12,8},{1,13},{5,1},{9,5},{13,9},{2,14},{6,2},{... | collective-permute-start | bytes 9437192 | tf_op jit(solution)/shard_map/ppermute | solution.py:43
  131.6 200.4 %collective-permute-start.2 = (bf16[16,6,64,256]{3,2,1,0:T(8,128)(2,1)}, bf16[16,6,64,256]{3,2,1,0:T(8,128)(2,1)}, u32[]{:S(2)}, u32[]{:S(2)}) collective-permute-start(bf16[16,6,64,256]{3,2,1,0:T(8,128)(2,1)} %collective-permute-done.1), channel_id=1, source_target_pairs={{0,4},{4,8},{8,12},{12,0},{1,5},{5,9},{9,13},{13,1},{2,6},{6,10},{... | collective-permute-start | bytes 9437192 | tf_op jit(solution)/shard_map/ppermute | solution.py:41
  187.3 64.8 %copy-start = (bf16[16,6,384,256]{2,3,1,0:T(8,128)(2,1)}, bf16[16,6,384,256]{2,3,1,0:T(8,128)(2,1)S(1)}, u32[]{:S(2)}) copy-start(bf16[16,6,384,256]{2,3,1,0:T(8,128)(2,1)S(1)} %broadcast_select_fusion) | copy-start | bytes 56623108
  361.0 4.2 copy-start.1
  361.0 5.0 copy-start.6
  366.0 4.2 copy-start.5
  372.8 251.6 %all-gather.14.cloned.1.call-start = ((), (), s32[]{:S(2)}) async-start(), calls=%async_computation.8 | async-start | bytes 15728640 | tf_op jit(solution)/shard_map/all_gather | solution.py:104
  373.4 392.2 %reduce-scatter.9.cloned.1.call-start = ((), (), s32[]{:S(2)}) async-start(), calls=%async_computation.12 | async-start | bytes 2621440 | tf_op jit(solution)/shard_map/reduce_scatter | solution.py:91
  408.8 359.2 %reduce-scatter.11.cloned.1.call-start = ((), (), s32[]{:S(2)}) async-start(), calls=%async_computation.13 | async-start | bytes 5242880 | tf_op jit(solution)/shard_map/reduce_scatter | solution.py:85
  413.2 396.8 %reduce-scatter.5.cloned.1.call-start = ((), (), s32[]{:S(2)}) async-start(), calls=%async_computation.9 | async-start | bytes 7864320 | tf_op jit(solution)/shard_map/reduce_scatter | solution.py:112
  749.8 1.9 copy-start.2
  749.8 274.3 %reduce-scatter.7.cloned.1.call-start = ((), (), s32[]{:S(2)}) async-start(), calls=%async_computation.11 | async-start | bytes 15728640 | tf_op jit(solution)/shard_map/reduce_scatter | solution.py:98
  765.5 44.5 %copy-start.4 = (bf16[2048,512]{1,0:T(8,128)(2,1)S(1)}, bf16[2048,512]{1,0:T(8,128)(2,1)}, u32[]{:S(2)}) copy-start(bf16[2048,512]{1,0:T(8,128)(2,1)} %all-gather.8.cloned.1.call-done) | copy-start | bytes 6291460
  765.5 44.5 %copy-start.7 = (bf16[384,512]{1,0:T(8,128)(2,1)S(1)}, bf16[384,512]{1,0:T(8,128)(2,1)}, u32[]{:S(2)}) copy-start(bf16[384,512]{1,0:T(8,128)(2,1)} %all-reduce.2.cloned.1.call-done) | copy-start | bytes 1179652
Sparse Core Ops, SparseCore 0:
  9.6 48.9 all-gather.7
  60.7 44.5 all-gather.5
  106.9 58.2 all-gather.9
  166.6 145.8 all-gather.11
  372.9 31.6 all-reduce.1
  406.1 218.2 all-gather.13
  627.4 41.9 reduce-scatter.8
  671.7 76.0 reduce-scatter.10
  751.1 58.8 reduce-scatter.4
  812.2 211.8 reduce-scatter.6
